TPU v7x, 256 devices: a whole 4x4x8 slice. The times are simulated.
256 devices in a mesh: mass: 32 (over z, x), rep: 8 (over y, core).
Axes of the slice: x: 4, y: 4, z: 8, core: 2. Of those that a mesh axis runs over, the one named last changes fastest.
Arguments:
- queries: bfloat16 [32768, 4096], P(('mass', 'rep'))
- library: bfloat16 [49152, 4096], P(('mass', 'rep'))
- windows: int32 [4096, 4], P(('mass', 'rep')), may hold values from 0 to 31, all different within a row; in each aligned block of 16 rows (0 to 15, 16 to 31, ...) at most 3 rows name the same one
Outputs:
- top_scores: float32 [32768, 128], P(('mass', 'rep'))
Inputs may be any that keep to these rules, and one draw needn't show every extreme that they name: `windows`: each row names 4 different shards. Among the 16 rows of one device no shard is named more than 3 times, a bound that some block reaches.
All inputs are finite; a program needn't handle non-finite values.
Results may differ from a plain program's by a relative error of at most 0.0015.
Values may be sent and summed in bfloat16 or wider, within the bound.
A program may use at most 128 MiB of HBM per device.

v0:
```python
import math

import jax
import jax.numpy as jnp
from jax import lax
from jax.sharding import PartitionSpec as P

K = 128


epsilon = 1e-06


def unit_rows(values):
    widened = values.astype(jnp.float32)
    inverse = lax.rsqrt(jnp.mean(widened * widened, axis=-1, keepdims=True) + epsilon)
    return (widened * inverse).astype(jnp.bfloat16)


def on_device(queries, library, windows):
    n_mass = lax.axis_size("mass")
    blocks, visit_width = windows.shape
    block_rows = queries.shape[0] // blocks
    bin_count = queries.shape[1]
    capacity = max(2, 3 * blocks * visit_width // (2 * n_mass))
    score_scale = 1.0 / math.sqrt(bin_count)
    visits = blocks * visit_width
    slot_count = n_mass * capacity
    targets = windows.reshape(visits)
    target_hits = (targets[:, None] == jnp.arange(n_mass, dtype=jnp.int32)[None, :]).astype(
        jnp.int32
    )
    ranking = jnp.sum((jnp.cumsum(target_hits, axis=0) - 1) * target_hits, axis=1)
    slot_index = targets * capacity + ranking
    owner_block = jnp.arange(visits, dtype=jnp.int32) // visit_width
    placing = (jnp.arange(slot_count, dtype=jnp.int32)[:, None] == slot_index[None, :]).astype(
        jnp.bfloat16
    )
    block_pick = (owner_block[:, None] == jnp.arange(blocks, dtype=jnp.int32)[None, :]).astype(
        jnp.bfloat16
    )
    selector = jnp.dot(placing, block_pick, preferred_element_type=jnp.float32).astype(jnp.bfloat16)
    unit_blocks = unit_rows(queries).reshape(blocks, block_rows * bin_count)
    outgoing = jnp.dot(selector, unit_blocks, preferred_element_type=jnp.float32).astype(
        jnp.bfloat16
    )
    outgoing = outgoing.reshape(n_mass, capacity * block_rows, bin_count)
    incoming = lax.all_to_all(outgoing, "mass", split_axis=0, concat_axis=0, tiled=True)
    slot_rows = incoming.reshape(slot_count * block_rows, bin_count)
    library_unit = unit_rows(library)
    scores = (
        jnp.einsum(
            "qf,lf->ql",
            slot_rows,
            lax.all_gather(library_unit, "rep", axis=0, tiled=True),
            preferred_element_type=jnp.float32,
        )
        * score_scale
    )
    best_scores = lax.top_k(scores, K)[0]
    returned = lax.all_to_all(
        best_scores.reshape(n_mass, capacity * block_rows, K),
        "mass",
        split_axis=0,
        concat_axis=0,
        tiled=True,
    )
    per_slot = returned.reshape(slot_count, block_rows, K)
    fetched = per_slot[slot_index].reshape(blocks, visit_width, block_rows, K)
    merged = jnp.transpose(fetched, (0, 2, 1, 3)).reshape(blocks * block_rows, visit_width * K)
    return lax.top_k(merged, K)[0]


def solution(mesh):
    placed = (P(("mass", "rep"), None), P(("mass", "rep"), None), P(("mass", "rep"), None))
    return jax.shard_map(
        on_device, mesh=mesh, in_specs=placed, out_specs=P(("mass", "rep"), None), check_vma=False
    )
```

profile of v0, /device:TPU:1, one launch (start us, length us, event | category | flops | bytes accessed | tf_op | source)
XLA Modules:
  0.0 456.8 jit_solution(9319652544158769971)
XLA Ops:
  6.5 0.0 copy-start.1
  6.5 0.0 copy-start
  6.5 0.0 all-gather.2.cloned.1.call-start
  6.5 1.9 fusion
  8.4 3.0 fusion.1
  11.5 0.0 all-gather.2.cloned.1.call-update
  11.5 0.0 copy-done.1
  11.5 0.1 copy.6
  11.6 0.1 reshape.90
  11.7 0.0 copy-done
  11.7 0.3 fusion.2
  12.0 0.3 fusion.3
  12.3 0.5 reshape.91
  12.8 0.1 fusion.4
  12.9 0.1 reduce_window_sum.11
  13.0 0.2 select_reduce_fusion
  13.2 4.0 convolution_convert_fusion
  17.2 10.4 %reshape.92 = bf16[32,24,4096]{2,1,0:T(8,128)(2,1)} reshape(bf16[96,32768]{1,0:T(8,128)(2,1)} %convolution_convert_fusion) | data formatting | bytes 12582912 | tf_op jit(solution)/shard_map/reshape | solution.py:47
  27.6 150.7 %all_to_all.10 = bf16[32,24,4096]{2,1,0:T(8,128)(2,1)} all-to-all(bf16[32,24,4096]{2,1,0:T(8,128)(2,1)} %reshape.92), channel_id=1, replica_groups=mesh['mass'=32,'rep'=8] {'mass'}, dimensions={0} | all-to-all | bytes 12582912 | tf_op jit(solution)/shard_map/all_to_all | solution.py:48
  178.3 0.0 all-gather.2.cloned.1.call-done
  178.3 16.3 %convolution_multiply_fusion = f32[768,1536]{1,0:T(8,128)} fusion(bf16[768,4096]{1,0:T(8,128)(2,1)} %bitcast.17, bf16[1536,4096]{1,0:T(8,128)(2,1)} %all-gather.2.cloned.1.call-done), kind=kOutput, calls=%fused_computation.2 | convolution fusion | flops 9664856064 | bytes 23592960 | tf_op jit(solution)/shard_map/qf,lf->ql/dot_general | solution.py:52
  194.7 6.0 %copy.8 = f32[768,1536]{0,1:T(8,128)} copy(f32[768,1536]{1,0:T(8,128)} %convolution_multiply_fusion) | data formatting | bytes 9437184
  200.7 2.5 iota.24.clone
  203.2 210.4 %top_k.14 = (f32[768,1536]{0,1:T(8,128)}, s32[768,1536]{0,1:T(8,128)}) sort(f32[768,1536]{0,1:T(8,128)} %copy.8, s32[768,1536]{0,1:T(8,128)} %iota.24.clone), dimensions={1}, to_apply=%region_4.5 | sort | flops 24772608 | bytes 18874368 | tf_op jit(solution)/shard_map/top_k | solution.py:60
  413.6 6.1 %copy.10 = f32[768,1536]{1,0:T(8,128)} copy(f32[768,1536]{0,1:T(8,128)} %get-tuple-element.11) | data formatting | bytes 9437184 | tf_op jit(solution)/shard_map/top_k | solution.py:60
  419.7 1.8 top_k.22
  421.5 6.6 %all-to-all-start.1 = ((f32[32,24,128]{2,1,0:T(8,128)}), f32[32,24,128]{2,1,0:T(8,128)S(1)}, u32[]{:S(2)}, u32[]{:S(2)}) async-start(f32[32,24,128]{2,1,0:T(8,128)} %bitcast.1), calls=%async_computation.1 | async-start | bytes 786432 | tf_op jit(solution)/shard_map/all_to_all | solution.py:61
  428.1 0.1 copy.7
  428.2 0.1 mul.65
  428.3 12.4 %all-to-all-done.1 = f32[32,24,128]{2,1,0:T(8,128)S(1)} async-done(((f32[32,24,128]{2,1,0:T(8,128)}), f32[32,24,128]{2,1,0:T(8,128)S(1)}, u32[]{:S(2)}, u32[]{:S(2)}) %all-to-all-start.1) | async-done | bytes 393248 | tf_op jit(solution)/shard_map/all_to_all | solution.py:61
  440.6 0.6 gather_fusion
  441.3 0.1 copy.12
  441.4 7.8 %top_k.20 = (f32[128,512]{0,1:T(8,128)S(1)}, s32[128,512]{0,1:T(8,128)}) sort(f32[128,512]{0,1:T(8,128)S(1)} %copy.12, s32[128,512]{0,1:T(8,128)S(1)} %iota.25.clone), dimensions={1}, to_apply=%region_5.6 | sort | flops 1048576 | bytes 1048576 | tf_op jit(solution)/shard_map/top_k | solution.py:71
  449.2 0.1 copy.14
  449.4 0.6 top_k.23
  (7 shorter events, 0.1 us)
Async XLA Ops:
  6.5 5.0 %copy-start.1 = (s32[16,4]{0,1:T(4,128)S(1)}, s32[16,4]{0,1:T(4,128)}, u32[]{:S(2)}) copy-start(s32[16,4]{0,1:T(4,128)} %param.5) | copy-start | bytes 772
  6.5 5.1 %copy-start = (bf16[128,4096]{1,0:T(8,128)(2,1)S(1)}, bf16[128,4096]{1,0:T(8,128)(2,1)}, u32[]{:S(2)}) copy-start(bf16[128,4096]{1,0:T(8,128)(2,1)} %param.3) | copy-start | bytes 3145732
  6.5 171.8 %all-gather.2.cloned.1.call-start = ((), (), s32[]{:S(2)}) async-start(), calls=%async_computation.2 | async-start | bytes 14155776 | tf_op jit(solution)/shard_map/all_gather | solution.py:55
  421.5 19.2 %all-to-all-start.1 = ((f32[32,24,128]{2,1,0:T(8,128)}), f32[32,24,128]{2,1,0:T(8,128)S(1)}, u32[]{:S(2)}, u32[]{:S(2)}) async-start(f32[32,24,128]{2,1,0:T(8,128)} %bitcast.1), calls=%async_computation.1 | async-start | bytes 786432 | tf_op jit(solution)/shard_map/all_to_all | solution.py:61
Sparse Core Ops, SparseCore 0:
  11.6 74.1 all-gather.1
where the time goes:
time: 461 us; the launch traced here: 457 us
  other arithmetic  224 us (49%)
  blocking collectives  151 us (33%)
  local copies, waits for them, and re-layouts  29.2 us (6%)
  matrix products  20.4 us (4%)
  between operations  13.5 us (3%)
  waiting for transfers between devices  12.4 us (3%)
  starting transfers between devices  6.58 us (1%)
    top_k x1, other arithmetic, on_device(): best_scores = lax.top_k(scores, K)[0]  210 us
    all_to_all x1, blocking collectives, on_device(): lax.all_to_all(outgoing, 'mass', split_axis=0, concat_axis=0, tiled=True)  151 us
    dot_general x1, matrix products, on_device(): jnp.einsum('qf,lf->ql', slot_rows, lax.all_gather(library_unit, 'rep', ax...  16.3 us
    all_to_all x1, waiting for transfers between devices, on_device(): lax.all_to_all(best_scores.reshape(n_mass, capacity * block_rows, K), 'ma...  12.4 us
    reshape x1, local copies, waits for them, and re-layouts, on_device(): outgoing = outgoing.reshape(n_mass, capacity * block_rows, bin_count)  10.4 us
  transfers between devices with their start and end apart: 2, of which 1 were waited for; matrix products, arithmetic and copies ran while one was open for 4% of the time, Pallas kernels for 0%

commit v1 on v0

v1 whole, which is shorter than its diff:
```python
import math

import jax
import jax.numpy as jnp
from jax import lax
from jax.experimental import pallas as pl
from jax.experimental.pallas import tpu as pltpu
from jax.sharding import PartitionSpec as P

MESH = pl.DeviceIdType.MESH
NZ, NX, NY = 8, 4, 4
BINS = 4096
HALF, QUARTER = BINS // 2, BINS // 4
QB = 8
BLOCKS = 16
TOPW = 4
CAP = 3
K = 128
ENTRIES = 192
SHARD = 1536
SLOT = 2 * QB
UNIT = CAP * SLOT
SLOTS = NX * CAP * QB
epsilon = 1e-06

OFFSET = (0, -1, 1, -2, 2, -3, 3, -4)
PIECES = [(s, a, b, p) for s, a, b in ((1, 0, 1), (-1, 0, 2), (1, 1, 3), (-1, 2, 4), (1, 3, 5)) for p in (0, 1)]
LAST = {10: (-1, 4, 6, 0), 11: (-1, 4, 6, 1), 12: (1, 5, 7, 0), 13: (1, 5, 7, 1)}
CODES = ((1, 1, 1), (-1, -1, 2), (2, 2, 3), (-2, -2, 4), (3, 3, 5), (-2, -3, 6), (3, 4, 7))


def at_index(v, i, axis):
    return lax.index_in_dim(v, i, axis, keepdims=False)


def paired(a, b, axis, up):
    hi, lo = jnp.maximum(a, b), jnp.minimum(a, b)
    return jnp.stack([lo, hi] if up else [hi, lo], axis=axis)


def clean(v, top, low, up=False):
    shape = v.shape
    s = top
    while s >= low:
        w = v.reshape((shape[0] // (2 * s), 2, s) + shape[1:])
        v = paired(at_index(w, 0, 1), at_index(w, 1, 1), 1, up).reshape(shape)
        s //= 2
    return v


def batcher(v):
    n = v.shape[0]
    shape = v.shape
    p = 1
    while p < n:
        k = p
        while k >= 1:
            w = v.reshape((n // (2 * p), 2 * p // k, k) + shape[1:])
            if k == p:
                w = paired(at_index(w, 0, 1), at_index(w, 1, 1), 1, False)
            else:
                c = 2 * p // k
                mid = lax.slice_in_dim(w, 1, c - 1, axis=1)
                mid = mid.reshape((n // (2 * p), (c - 2) // 2, 2, k) + shape[1:])
                mid = paired(at_index(mid, 0, 2), at_index(mid, 1, 2), 2, False)
                mid = mid.reshape((n // (2 * p), c - 2, k) + shape[1:])
                w = jnp.concatenate([lax.slice_in_dim(w, 0, 1, axis=1), mid, lax.slice_in_dim(w, c - 1, c, axis=1)], axis=1)
            v = w.reshape(shape)
            k //= 2
        p *= 2
    return v


def backwards(v):
    n = v.shape[0]
    return jnp.concatenate([lax.slice_in_dim(v, n - 1 - i, n - i, axis=0) for i in range(n)], axis=0)


def repeat(count, body, unroll=True):
    def step(i, carry):
        body(i)
        return carry
    lax.fori_loop(0, count, step, 0, unroll=unroll)


def coarse(ref, base, n, top, low, i, width, up=False):
    v = jnp.stack([ref[pl.ds(base + n * j + i, width)] for j in range(8)], axis=0)
    v = clean(v, top, low, up)
    for j in range(8):
        ref[pl.ds(base + n * j + i, width)] = at_index(v, j, 0)


def fine(ref, base, n, groups, i, up=False):
    at = pl.ds(base + i * n * groups, n * groups)
    ref[at] = clean(ref[at], n // 2, 1, up)


def across(ref, shift):
    def body(i):
        i = i * 4
        a = jnp.stack([ref[pl.ds(16 * j + i, 4)] for j in range(8)], axis=0)
        r = jnp.stack([ref[pl.ds(16 * j + 12 - i, 4)] for j in range(8)], axis=0)
        flat = (32, 8, 128)
        ra = backwards(r.reshape(flat))
        rr = backwards(a.reshape(flat))
        a = jnp.maximum(a.reshape(flat), pltpu.roll(ra, shift, 1)).reshape(8, 4, 8, 128)
        r = jnp.maximum(r.reshape(flat), pltpu.roll(rr, shift, 1)).reshape(8, 4, 8, 128)
        a, r = clean(a, 4, 1), clean(r, 4, 1)
        for j in range(8):
            ref[pl.ds(16 * j + i, 4)] = at_index(a, j, 0)
            ref[pl.ds(16 * j + 12 - i, 4)] = at_index(r, j, 0)
    repeat(2, body)


def collect(ref, o_ref):
    own = lax.broadcasted_iota(jnp.int32, (1, 8, 8, 128), 1) == lax.broadcasted_iota(jnp.int32, (1, 8, 8, 128), 2)
    def body(g):
        v = clean(ref[pl.ds(g * 32, 32)], 8, 1).reshape(4, 8, 8, 128)
        o_ref[pl.ds(pl.multiple_of(g * 32, 32), 32), :] = jnp.sum(jnp.where(own, v, 0.0), axis=1).reshape(32, 128)
    repeat(4, body)


def top_rows(ref, o_ref):
    def sort32(c):
        for up in (0, 1):
            at = pl.ds((c * 2 + up) * 32, 32)
            v = batcher(ref[at])
            ref[at] = backwards(v) if up else v
    repeat(3, sort32, False)
    for c in range(3):
        repeat(2, lambda i: coarse(ref, c * 64, 8, 4, 1, i * 4, 4, c > 0))
        repeat(2, lambda i: fine(ref, c * 64, 8, 4, i, c > 0))
    def third(i):
        i = i * 4
        v = [ref[pl.ds(16 * j + i, 4)] for j in range(8)]
        for j in range(4, 8):
            v[j] = jnp.maximum(v[j], ref[pl.ds(16 * j + 64 + i, 4)])
        v = clean(jnp.stack(v, axis=0), 4, 1)
        for j in range(8):
            ref[pl.ds(16 * j + i, 4)] = at_index(v, j, 0)
    repeat(4, lambda i: coarse(ref, 0, 16, 4, 1, i * 4, 4))
    repeat(4, lambda i: fine(ref, 0, 16, 2, i))
    repeat(4, third)
    repeat(4, lambda i: fine(ref, 0, 16, 2, i))
    for shift in (4, 2, 1):
        across(ref, shift)
        if shift != 1:
            repeat(4, lambda i: fine(ref, 0, 16, 2, i))
    collect(ref, o_ref)


def kernel(
    q_hbm, l_hbm, w_ref, o_ref,
    q_in, l_in, chunk, packed, arrived, rows, lib, scores, best, outgoing, incoming, code_own, code_in, slot_of, lists, mixed,
    load_sem, zs, zr, xs, xr, cs, cr, ys, yr, ks, kr, rs, rr,
):
    m, r = lax.axis_index("mass"), lax.axis_index("rep")
    z, x, y, c = m // NX, m % NX, r // 2, r % 2
    sign = 2 * c - 1

    def mass_at(dz, dx):
        return (z + dz * sign + NZ) % NZ * NX + (x + dx) % NX

    def remote(src, dst, send, recv, device):
        return pltpu.make_async_remote_copy(
            src_ref=src, dst_ref=dst, send_sem=send, recv_sem=recv, device_id=device, device_id_type=MESH
        )

    def y_rep(dy, core):
        return (y + dy * sign + NY) % NY * 2 + core

    load_q = pltpu.make_async_copy(q_hbm, q_in, load_sem.at[0])
    load_l = pltpu.make_async_copy(l_hbm, l_in, load_sem.at[1])
    load_q.start()
    load_l.start()

    barrier = pltpu.get_barrier_semaphore()

    def greet(i):
        pl.semaphore_signal(barrier, inc=1, device_id=((m + i + 1) % (NZ * NX), r), device_id_type=MESH)

    repeat(NZ * NX - 1, greet, False)
    for dy in (1, 2, 3):
        pl.semaphore_signal(barrier, inc=1, device_id=(m, y_rep(dy, c)), device_id_type=MESH)
    pl.semaphore_signal(barrier, inc=1, device_id=(m, y * 2 + 1 - c), device_id_type=MESH)

    def unit(values):
        widened = values.astype(jnp.float32)
        inverse = lax.rsqrt(jnp.mean(widened * widened, axis=-1, keepdims=True) + epsilon)
        return widened * inverse

    load_q.wait()

    def own_rows(i):
        two = unit(q_in[pl.ds(pl.multiple_of(i * 16, 16), 16), :])
        for b in (0, 1):
            u = two[b * 8 : b * 8 + 8]
            for p in (0, 1):
                halves = [u[:, p * HALF + h * QUARTER : p * HALF + (h + 1) * QUARTER] for h in (0, 1)]
                at = pl.ds(pl.multiple_of((i * 2 + b) * SLOT, SLOT), SLOT)
                chunk[0, p, at, :] = jnp.concatenate(halves, axis=0).astype(jnp.bfloat16)

    repeat(8, own_rows, False)

    lane_block = lax.broadcasted_iota(jnp.int32, (1, 256), 1) // SLOT
    shard_id = lax.broadcasted_iota(jnp.int32, (64, 256), 0)
    shard_id = shard_id // 8 * NX + shard_id % NX
    hit = jnp.zeros((64, 256), jnp.float32)
    for v in range(TOPW):
        named = jnp.zeros((1, 256), jnp.int32)
        for b in range(BLOCKS):
            named = jnp.where(lane_block == b, w_ref[b, v], named)
        hit = jnp.where(shard_id == named, 1.0, hit)
    before = lax.broadcasted_iota(jnp.int32, (256, 256), 0)
    after = lax.broadcasted_iota(jnp.int32, (256, 256), 1) // SLOT
    earlier = jnp.where((before // SLOT < after) & (before % SLOT == 0), 1.0, 0.0).astype(jnp.bfloat16)
    count = jnp.dot(hit.astype(jnp.bfloat16), earlier, preferred_element_type=jnp.float32)
    code = jnp.where(hit > 0.5, count, -1.0)
    for plane in range(NZ):
        code_own[plane] = code[plane * 8 : plane * 8 + 8]

    pl.semaphore_wait(barrier, NZ * NX - 1 + NY - 1 + 1)

    codes = {}
    for dz, dp, k in CODES:
        codes[k] = remote(
            code_own.at[(z + dp * sign + NZ) % NZ], code_in.at[k], cs.at[k], cr.at[k], (mass_at(dz, 0), r)
        )
        codes[k].start()

    ring = []
    for n, (s, a, b, p) in enumerate(PIECES):
        ring.append(remote(chunk.at[a, p], chunk.at[b, p], zs.at[n], zr.at[n], (mass_at(s, 0), r)))
    for n in (0, 1):
        ring[n].start()

    load_l.wait()

    def own_entries(i):
        at = pl.multiple_of(i * 16, 16)
        lib[pl.ds(pl.multiple_of(r * ENTRIES + at, 16), 16), :] = unit(l_in[pl.ds(at, 16), :]).astype(jnp.bfloat16)

    repeat(ENTRIES // 16, own_entries, False)

    def entries(rep, part=None):
        first, size = (0, ENTRIES) if part is None else (part * (ENTRIES // 2), ENTRIES // 2)
        return lib.at[pl.ds(pl.multiple_of(rep * ENTRIES + first, 16), size)]

    def along_y(n, rep, dy, part=None):
        return remote(entries(rep, part), entries(rep, part), ys.at[n], yr.at[n], (m, y_rep(dy, c)))

    def to_sibling(n, rep):
        return remote(entries(rep), entries(rep), ks.at[n], kr.at[n], (m, y * 2 + 1 - c))

    lib_y = [along_y(0, r, 1), along_y(1, r, -1), along_y(2, y_rep(-1, c), 1, 0), along_y(3, y_rep(1, c), -1, 1)]
    lib_c = [to_sibling(n, y_rep(dy, c)) for n, dy in enumerate((0, -1, 1, 2))]
    lib_y[0].start()
    lib_c[0].start()

    diagonal = lax.broadcasted_iota(jnp.int32, (SLOT, 256), 1) % SLOT == lax.broadcasted_iota(jnp.int32, (SLOT, 256), 0)

    def pick(k, p, held):
        parts = []
        for d in range(NX):
            at = pl.ds((x + d) % NX, 1)
            line = code_own[z, at, :] if k == 0 else code_in[k, at, :]
            for slot in range(CAP):
                parts.append(jnp.where(diagonal & (line == float(slot)), 1.0, 0.0))
        select = jnp.concatenate(parts, axis=0).astype(jnp.bfloat16)
        for t in range(QUARTER // 256):
            at = pl.ds(t * 256, 256)
            out = jnp.dot(select, chunk[held, p, :, at], preferred_element_type=jnp.float32).astype(jnp.bfloat16)
            for d in range(NX):
                part = out[d * UNIT : (d + 1) * UNIT]
                if d == 0 and k < 6:
                    arrived[k, p, 0, :, at] = part
                else:
                    packed[k, p, d, :, at] = part

    hops = {}
    for k in range(8):
        dz = {6: -1, 7: 1}.get(k, 0)
        for p in (0, 1):
            for d in range(NX):
                if d or k >= 6:
                    hops[k, p, d] = remote(
                        packed.at[k, p, d], arrived.at[k, p, d], xs.at[k, p, d], xr.at[k, p, d], (mass_at(dz, d), r)
                    )

    def send(k, p):
        for d in range(NX):
            if (k, p, d) in hops:
                hops[k, p, d].start()

    def unpack(k):
        for p in (0, 1):
            for d in range(NX):
                if (k, p, d) in hops:
                    hops[k, p, d].wait_recv()
        for p in (0, 1):
            for j in range(NX * CAP // 2):
                two = []
                for s in (2 * j, 2 * j + 1):
                    at = pl.ds(s % CAP * SLOT, SLOT)
                    two.append(arrived[k, p, s // CAP, at, :].astype(jnp.float32))
                for h in (0, 1):
                    block = jnp.concatenate([v[h * 8 : h * 8 + 8] for v in two], axis=0).astype(jnp.bfloat16)
                    first = p * HALF + h * QUARTER
                    rows[k * SLOTS + j * 16 : k * SLOTS + j * 16 + 16, first : first + QUARTER] = block

    def score(group, groups, rep):
        at = pl.ds(pl.multiple_of(rep * ENTRIES, 16), ENTRIES)
        out = lax.dot_general(
            lib[at, :],
            rows[group * 128 : (group + groups) * 128, :],
            (((1,), (1,)), ((), ())),
            preferred_element_type=jnp.float32,
        )
        for g in range(groups):
            part = out[:, g * 128 : g * 128 + 128].reshape(ENTRIES // 8, 8, 128)
            scores[group + g, pl.ds(rep * (ENTRIES // 8), ENTRIES // 8)] = part

    returns = {}
    for k in range(8):
        for d in range(NX):
            if k or d:
                at = pl.ds(k * SLOTS + d * CAP * QB, CAP * QB)
                returns[k, d] = remote(
                    outgoing.at[at], incoming.at[m], rs.at[k, d], rr.at[k, d], (mass_at(OFFSET[k], NX - d), r)
                )

    def choose(group):
        top_rows(scores.at[group], best)
        outgoing[group * 128 : group * 128 + 128, :] = best[...].T

    def give_back(k):
        for d in range(NX):
            if k or d:
                returns[k, d].start()
            else:
                incoming[m] = outgoing[0 : CAP * QB, :]

    pick(0, 0, 0)
    send(0, 0)
    pick(0, 1, 0)
    send(0, 1)

    for b in range(BLOCKS):
        for v in range(TOPW):
            shard = w_ref[b, v]
            line = code_own[shard // NX, pl.ds(shard % NX, 1), :]
            slot_of[b, v] = jnp.broadcast_to(line[:, b * SLOT : b * SLOT + 1], (8, 128))

    quarter = [
        (r, y * 2 + 1 - c),
        (y_rep(-1, c), y_rep(1, 1 - c)),
        (y_rep(1, c), y_rep(-1, 1 - c)),
        (y_rep(2, c), y_rep(2, 1 - c)),
    ]

    def score_quarters(group, groups, which):
        for i in which:
            for rep in quarter[i]:
                score(group, groups, rep)

    def score_all(group, groups):
        repeat(2 * NY, lambda rep: score(group, groups, rep), False)

    for n in range(14):
        if n < 10:
            ring[n].wait_send()
        else:
            k, p = LAST[n][2], LAST[n][3]
            for d in range(NX):
                hops[k, p, d].wait_send()
        if n + 2 < 10:
            ring[n + 2].start()
        elif n + 2 < 14:
            send(LAST[n + 2][2], LAST[n + 2][3])
        if n < 10:
            ring[n].wait_recv()
            b, p = PIECES[n][2], PIECES[n][3]
            if p == 0:
                codes[b].wait_recv()
            pick(b, p, b)
            send(b, p)
            if b in (4, 5):
                if p == 0:
                    codes[b + 2].wait_recv()
                pick(b + 2, p, b)
        if n == 2:
            lib_y[0].wait_send()
            lib_y[1].start()
            unpack(0)
            unpack(1)
        elif n == 3:
            lib_y[0].wait_recv()
            lib_c[1].start()
            lib_c[0].wait_recv()
        elif n == 4:
            unpack(2)
            lib_c[1].wait_recv()
            score_quarters(0, 2, (0, 1))
        elif n == 5:
            lib_y[1].wait_send()
            lib_y[2].start()
        elif n == 6:
            lib_y[1].wait_recv()
            lib_y[3].start()
            lib_c[2].start()
            unpack(3)
            score_quarters(2, 1, (0, 1))
        elif n == 7:
            lib_c[2].wait_recv()
            score_quarters(0, 2, (2,))
            score_quarters(2, 1, (2,))
        elif n == 8:
            unpack(4)
        elif n == 9:
            lib_y[2].wait_recv()
            lib_y[3].wait_recv()
            lib_c[3].start()
            lib_c[3].wait_recv()
            score_quarters(0, 2, (3,))
            choose(0)
            give_back(0)
            choose(1)
            give_back(1)
        elif n == 10:
            unpack(5)
            score_quarters(2, 1, (3,))
            choose(2)
            give_back(2)
            give_back(3)
            score_all(3, 1)
        elif n == 11:
            choose(3)
            give_back(4)
        elif n == 12:
            unpack(6)
            score_all(4, 1)
            choose(4)
            give_back(5)
    unpack(7)
    score_all(5, 1)
    choose(5)
    give_back(6)
    give_back(7)

    for k, d in returns:
        returns[k, d].wait_recv()

    def fetch(b):
        for v in range(TOPW):
            shard, slot = w_ref[b, v], slot_of[b, v]
            found = [incoming[shard, i * QB : i * QB + QB, :] for i in range(CAP)]
            found = jnp.where(slot < 0.5, found[0], jnp.where(slot < 1.5, found[1], found[2]))
            lists[v, pl.ds(pl.multiple_of(b * QB, QB), QB), :] = found

    repeat(BLOCKS, fetch, 4)
    for v in range(TOPW):
        lists[v] = lists[v].T
    sub = lax.broadcasted_iota(jnp.int32, (8, 128), 0) % TOPW

    def mix(i):
        line = [lists[v, pl.ds(i, 1), :] for v in range(TOPW)]
        mixed[i] = jnp.where(sub == 0, line[0], jnp.where(sub == 1, line[1], jnp.where(sub == 2, line[2], line[3])))

    repeat(K, mix, 16)
    across(mixed, 2)
    repeat(4, lambda i: fine(mixed, 0, 16, 2, i))
    across(mixed, 1)
    collect(mixed, best)
    o_ref[...] = best[...].T

    for copy in codes.values():
        copy.wait_send()
    for k in range(6):
        for p in (0, 1):
            for d in range(1, NX):
                hops[k, p, d].wait_send()
    for n in (2, 3):
        lib_y[n].wait_send()
    for copy in lib_c:
        copy.wait_send()
    for copy in returns.values():
        copy.wait_send()


def on_device(queries, library, windows):
    bf16, f32, dma = jnp.bfloat16, jnp.float32, pltpu.SemaphoreType.DMA
    scores = pl.pallas_call(
        kernel,
        out_shape=jax.ShapeDtypeStruct((BLOCKS * QB, K), f32),
        in_specs=[
            pl.BlockSpec(memory_space=pl.ANY),
            pl.BlockSpec(memory_space=pl.ANY),
            pl.BlockSpec(memory_space=pltpu.SMEM),
        ],
        out_specs=pl.BlockSpec(memory_space=pltpu.VMEM),
        scratch_shapes=[
            pltpu.VMEM((BLOCKS * QB, BINS), bf16),
            pltpu.VMEM((ENTRIES, BINS), bf16),
            pltpu.VMEM((6, 2, BLOCKS * SLOT, QUARTER), bf16),
            pltpu.VMEM((8, 2, NX, UNIT, QUARTER), bf16),
            pltpu.VMEM((8, 2, NX, UNIT, QUARTER), bf16),
            pltpu.VMEM((8 * SLOTS, BINS), bf16),
            pltpu.VMEM((SHARD, BINS), bf16),
            pltpu.VMEM((6, SHARD // 8, 8, 128), f32),
            pltpu.VMEM((128, 128), f32),
            pltpu.VMEM((8 * SLOTS, K), f32),
            pltpu.VMEM((NZ * NX, CAP * QB, K), f32),
            pltpu.VMEM((NZ, 8, 256), f32),
            pltpu.VMEM((8, 8, 256), f32),
            pltpu.VMEM((BLOCKS, TOPW, 8, 128), f32),
            pltpu.VMEM((TOPW, 128, K), f32),
            pltpu.VMEM((K, 8, 128), f32),
            dma((2,)),
            dma((10,)),
            dma((10,)),
            dma((8, 2, NX)),
            dma((8, 2, NX)),
            dma((8,)),
            dma((8,)),
            dma((4,)),
            dma((4,)),
            dma((4,)),
            dma((4,)),
            dma((8, NX)),
            dma((8, NX)),
        ],
        compiler_params=pltpu.CompilerParams(
            collective_id=0, has_side_effects=True, vmem_limit_bytes=60 * 2**20
        ),
    )(queries, library, windows)
    return scores * (1.0 / math.sqrt(BINS))


def solution(mesh):
    placed = (P(("mass", "rep"), None), P(("mass", "rep"), None), P(("mass", "rep"), None))
    return jax.shard_map(
        on_device, mesh=mesh, in_specs=placed, out_specs=P(("mass", "rep"), None), check_vma=False
    )
```

time: 461 us -> 125 us (0.27)
  other arithmetic: 224 us -> 1.48 us
  blocking collectives: 151 us -> 0 us
  Pallas kernels: 0 us -> 121 us
  local copies, waits for them, and re-layouts: 29.2 us -> 1.35 us
  matrix products: 20.4 us -> 0 us
  between operations: 13.5 us -> 0.01 us
  waiting for transfers between devices: 12.4 us -> 0 us
  starting transfers between devices: 6.58 us -> 0 us
    top_k x2 -> x0, other arithmetic: 218 us -> none  [the longest x1 210 us: on_device(): best_scores = lax.top_k(scores, K)[0]]
    all_to_all x1 -> x0, blocking collectives: 151 us -> none  [on_device(): lax.all_to_all(outgoing, 'mass', split_axis=0, concat_axis=0, tiled=True)]
    pallas_call x0 -> x1, Pallas kernels: none -> 121 us  [on_device(): pl.pallas_call(kernel, out_shape=jax.ShapeDtypeStruct((BLOCKS * QB, K), f...]
    dot_general x2 -> x0, matrix products: 20.4 us -> none  [the longest x1 16.3 us: on_device(): jnp.einsum('qf,lf->ql', slot_rows, lax.all_gather(library_unit, 'rep', ax...]
    all_to_all x1 -> x0, waiting for transfers between devices: 12.4 us -> none  [on_device(): lax.all_to_all(best_scores.reshape(n_mass, capacity * block_rows, K), 'ma...]
    reshape x3 -> x0, local copies, waits for them, and re-layouts: 11 us -> none  [the longest x1 10.4 us: on_device(): outgoing = outgoing.reshape(n_mass, capacity * block_rows, bin_count)]
    top_k x4 -> x0, local copies, waits for them, and re-layouts: 8.65 us -> none  [the longest x2 7.89 us: on_device(): best_scores = lax.top_k(scores, K)[0]]
    all_to_all x1 -> x0, starting transfers between devices: 6.58 us -> none  [on_device(): lax.all_to_all(best_scores.reshape(n_mass, capacity * block_rows, K), 'ma...]
  transfers between devices with their start and end apart: 2 -> 0, of which waited for: 1 -> 0; matrix products, arithmetic and copies ran while one was open for 4% -> 0% of each run, Pallas kernels for 0% -> 0%
where the time goes in v1:
time: 125 us; the launch traced here: 123 us
  Pallas kernels  121 us (97%)
  other arithmetic  1.48 us (1%)
  local copies, waits for them, and re-layouts  1.35 us (1%)
    pallas_call x1, Pallas kernels, on_device(): pl.pallas_call(kernel, out_shape=jax.ShapeDtypeStruct((BLOCKS * QB, K), f...  121 us

profile of v1, /device:TPU:1, one launch (start us, length us, event | category | flops | bytes accessed | tf_op | source)
XLA Modules:
  0.0 123.5 jit_solution(11125035781991975709)
XLA Ops:
  0.0 1.4 %copy.4.w_ref = s32[16,4]{1,0:T(8,128)} copy(s32[16,4]{0,1:T(4,128)} %param.5) | data formatting | bytes 512 | tf_op args[2]
  1.4 120.6 %shard_map.37 = f32[128,128]{1,0:T(8,128)} custom-call(bf16[128,4096]{1,0:T(8,128)(2,1)} %q_hbm.1, bf16[192,4096]{1,0:T(8,128)(2,1)} %l_hbm.1, s32[16,4]{1,0:T(8,128)} %copy.4.w_ref), custom_call_target="tpu_custom_call" | custom-call | tf_op jit(solution)/shard_map/pallas_call | solution.py:492
  122.0 1.5 %broadcast_multiply_fusion = f32[128,128]{1,0:T(8,128)} fusion(f32[128,128]{1,0:T(8,128)} %shard_map.37), kind=kLoop, calls=%fused_computation | loop fusion | flops 16384 | bytes 131072 | tf_op jit(solution)/shard_map/mul | solution.py:536

commit v2 on v1

--- a/solution.py
+++ b/solution.py
@@ -120,16 +120,26 @@
     repeat(4, body)
 
 
-def top_rows(ref, o_ref):
-    def sort32(c):
-        for up in (0, 1):
-            at = pl.ds((c * 2 + up) * 32, 32)
-            v = batcher(ref[at])
-            ref[at] = backwards(v) if up else v
-    repeat(3, sort32, False)
-    for c in range(3):
-        repeat(2, lambda i: coarse(ref, c * 64, 8, 4, 1, i * 4, 4, c > 0))
-        repeat(2, lambda i: fine(ref, c * 64, 8, 4, i, c > 0))
+def sort_part(ref, c):
+    def sort32(up):
+        at = pl.ds(c * 64 + up * 32, 32)
+        v = batcher(ref[at])
+        ref[at] = backwards(v) if up else v
+
+    for up in (0, 1):
+        sort32(up)
+    repeat(2, lambda i: coarse(ref, c * 64, 8, 4, 1, i * 4, 4, c > 0))
+    repeat(2, lambda i: fine(ref, c * 64, 8, 4, i, c > 0))
+
+
+def begin_rows(ref):
+    for c in (0, 1):
+        sort_part(ref, c)
+    repeat(4, lambda i: coarse(ref, 0, 16, 4, 1, i * 4, 4))
+    repeat(4, lambda i: fine(ref, 0, 16, 2, i))
+
+
+def end_rows(ref, o_ref):
     def third(i):
         i = i * 4
         v = [ref[pl.ds(16 * j + i, 4)] for j in range(8)]
@@ -138,8 +148,8 @@
         v = clean(jnp.stack(v, axis=0), 4, 1)
         for j in range(8):
             ref[pl.ds(16 * j + i, 4)] = at_index(v, j, 0)
-    repeat(4, lambda i: coarse(ref, 0, 16, 4, 1, i * 4, 4))
-    repeat(4, lambda i: fine(ref, 0, 16, 2, i))
+
+    sort_part(ref, 2)
     repeat(4, third)
     repeat(4, lambda i: fine(ref, 0, 16, 2, i))
     for shift in (4, 2, 1):
@@ -176,10 +186,10 @@
 
     barrier = pltpu.get_barrier_semaphore()
 
-    def greet(i):
-        pl.semaphore_signal(barrier, inc=1, device_id=((m + i + 1) % (NZ * NX), r), device_id_type=MESH)
-
-    repeat(NZ * NX - 1, greet, False)
+    for dz in (1, 2, 3, 5, 6, 7):
+        pl.semaphore_signal(barrier, inc=1, device_id=((z + dz) % NZ * NX + x, r), device_id_type=MESH)
+    for dx in (1, 2, 3):
+        pl.semaphore_signal(barrier, inc=1, device_id=(mass_at(0, dx), r), device_id_type=MESH)
     for dy in (1, 2, 3):
         pl.semaphore_signal(barrier, inc=1, device_id=(m, y_rep(dy, c)), device_id_type=MESH)
     pl.semaphore_signal(barrier, inc=1, device_id=(m, y * 2 + 1 - c), device_id_type=MESH)
@@ -209,7 +219,7 @@
     for v in range(TOPW):
         named = jnp.zeros((1, 256), jnp.int32)
         for b in range(BLOCKS):
-            named = jnp.where(lane_block == b, w_ref[b, v], named)
+            named = jnp.where(lane_block == b, w_ref[v, b], named)
         hit = jnp.where(shard_id == named, 1.0, hit)
     before = lax.broadcasted_iota(jnp.int32, (256, 256), 0)
     after = lax.broadcasted_iota(jnp.int32, (256, 256), 1) // SLOT
@@ -219,7 +229,7 @@
     for plane in range(NZ):
         code_own[plane] = code[plane * 8 : plane * 8 + 8]
 
-    pl.semaphore_wait(barrier, NZ * NX - 1 + NY - 1 + 1)
+    pl.semaphore_wait(barrier, 13)
 
     codes = {}
     for dz, dp, k in CODES:
@@ -231,8 +241,7 @@
     ring = []
     for n, (s, a, b, p) in enumerate(PIECES):
         ring.append(remote(chunk.at[a, p], chunk.at[b, p], zs.at[n], zr.at[n], (mass_at(s, 0), r)))
-    for n in (0, 1):
-        ring[n].start()
+    ring[0].start()
 
     load_l.wait()
 
@@ -241,6 +250,7 @@
         lib[pl.ds(pl.multiple_of(r * ENTRIES + at, 16), 16), :] = unit(l_in[pl.ds(at, 16), :]).astype(jnp.bfloat16)
 
     repeat(ENTRIES // 16, own_entries, False)
+    ring[1].start()
 
     def entries(rep, part=None):
         first, size = (0, ENTRIES) if part is None else (part * (ENTRIES // 2), ENTRIES // 2)
@@ -252,9 +262,17 @@
     def to_sibling(n, rep):
         return remote(entries(rep), entries(rep), ks.at[n], kr.at[n], (m, y * 2 + 1 - c))
 
-    lib_y = [along_y(0, r, 1), along_y(1, r, -1), along_y(2, y_rep(-1, c), 1, 0), along_y(3, y_rep(1, c), -1, 1)]
+    lib_y = [
+        along_y(0, r, 1, 0),
+        along_y(1, r, -1, 1),
+        along_y(2, r, 1, 1),
+        along_y(3, r, -1, 0),
+        along_y(4, y_rep(-1, c), 1, 0),
+        along_y(5, y_rep(1, c), -1, 1),
+    ]
     lib_c = [to_sibling(n, y_rep(dy, c)) for n, dy in enumerate((0, -1, 1, 2))]
     lib_y[0].start()
+    lib_y[1].start()
     lib_c[0].start()
 
     diagonal = lax.broadcasted_iota(jnp.int32, (SLOT, 256), 1) % SLOT == lax.broadcasted_iota(jnp.int32, (SLOT, 256), 0)
@@ -292,12 +310,12 @@
             if (k, p, d) in hops:
                 hops[k, p, d].start()
 
-    def unpack(k):
-        for p in (0, 1):
+    def unpack(k, pieces=(0, 1)):
+        for p in pieces:
             for d in range(NX):
                 if (k, p, d) in hops:
                     hops[k, p, d].wait_recv()
-        for p in (0, 1):
+        for p in pieces:
             for j in range(NX * CAP // 2):
                 two = []
                 for s in (2 * j, 2 * j + 1):
@@ -308,17 +326,18 @@
                     first = p * HALF + h * QUARTER
                     rows[k * SLOTS + j * 16 : k * SLOTS + j * 16 + 16, first : first + QUARTER] = block
 
-    def score(group, groups, rep):
-        at = pl.ds(pl.multiple_of(rep * ENTRIES, 16), ENTRIES)
+    def score(group, groups, first, size, place, part=None):
+        bins = slice(0, BINS) if part is None else slice(part * HALF, part * HALF + HALF)
         out = lax.dot_general(
-            lib[at, :],
-            rows[group * 128 : (group + groups) * 128, :],
+            lib[pl.ds(pl.multiple_of(first, 128), size), bins],
+            rows[group * 128 : (group + groups) * 128, bins],
             (((1,), (1,)), ((), ())),
             preferred_element_type=jnp.float32,
         )
+        at = pl.ds(place // 8, size // 8)
         for g in range(groups):
-            part = out[:, g * 128 : g * 128 + 128].reshape(ENTRIES // 8, 8, 128)
-            scores[group + g, pl.ds(rep * (ENTRIES // 8), ENTRIES // 8)] = part
+            new = out[:, g * 128 : g * 128 + 128].reshape(size // 8, 8, 128)
+            scores[group + g, at] = scores[group + g, at] + new if part else new
 
     returns = {}
     for k in range(8):
@@ -330,7 +349,7 @@
                 )
 
     def choose(group):
-        top_rows(scores.at[group], best)
+        end_rows(scores.at[group], best)
         outgoing[group * 128 : group * 128 + 128, :] = best[...].T
 
     def give_back(k):
@@ -347,24 +366,16 @@
 
     for b in range(BLOCKS):
         for v in range(TOPW):
-            shard = w_ref[b, v]
+            shard = w_ref[v, b]
             line = code_own[shard // NX, pl.ds(shard % NX, 1), :]
             slot_of[b, v] = jnp.broadcast_to(line[:, b * SLOT : b * SLOT + 1], (8, 128))
 
-    quarter = [
-        (r, y * 2 + 1 - c),
-        (y_rep(-1, c), y_rep(1, 1 - c)),
-        (y_rep(1, c), y_rep(-1, 1 - c)),
-        (y_rep(2, c), y_rep(2, 1 - c)),
-    ]
-
     def score_quarters(group, groups, which):
         for i in which:
-            for rep in quarter[i]:
-                score(group, groups, rep)
-
-    def score_all(group, groups):
-        repeat(2 * NY, lambda rep: score(group, groups, rep), False)
+            score(group, groups, (y + (0, NY - 1, 1, 2)[i]) % NY * 2 * ENTRIES, 2 * ENTRIES, i * 2 * ENTRIES)
+
+    def score_all(group, part=None):
+        repeat(2, lambda i: score(group, 1, i * (SHARD // 2), SHARD // 2, i * (SHARD // 2), part), False)
 
     for n in range(14):
         if n < 10:
@@ -389,60 +400,63 @@
                     codes[b + 2].wait_recv()
                 pick(b + 2, p, b)
         if n == 2:
-            lib_y[0].wait_send()
-            lib_y[1].start()
+            lib_y[2].start()
+            lib_y[3].start()
             unpack(0)
+        elif n == 3:
             unpack(1)
-        elif n == 3:
+        elif n == 4:
             lib_y[0].wait_recv()
+            lib_y[1].wait_recv()
+            lib_y[4].start()
+            lib_y[5].start()
+        elif n == 5:
+            unpack(2)
+        elif n == 6:
+            lib_y[2].wait_recv()
+            lib_y[3].wait_recv()
             lib_c[1].start()
+            lib_c[2].start()
             lib_c[0].wait_recv()
-        elif n == 4:
-            unpack(2)
+            score_quarters(0, 2, (0,))
+        elif n == 7:
+            unpack(3)
             lib_c[1].wait_recv()
-            score_quarters(0, 2, (0, 1))
-        elif n == 5:
-            lib_y[1].wait_send()
-            lib_y[2].start()
-        elif n == 6:
-            lib_y[1].wait_recv()
-            lib_y[3].start()
-            lib_c[2].start()
-            unpack(3)
-            score_quarters(2, 1, (0, 1))
-        elif n == 7:
             lib_c[2].wait_recv()
-            score_quarters(0, 2, (2,))
-            score_quarters(2, 1, (2,))
+            score_quarters(0, 2, (1, 2))
+            score_quarters(2, 1, (0, 1, 2))
         elif n == 8:
             unpack(4)
+            for group in (0, 1, 2):
+                begin_rows(scores.at[group])
         elif n == 9:
-            lib_y[2].wait_recv()
-            lib_y[3].wait_recv()
+            lib_y[4].wait_recv()
+            lib_y[5].wait_recv()
             lib_c[3].start()
             lib_c[3].wait_recv()
             score_quarters(0, 2, (3,))
             choose(0)
-            give_back(0)
             choose(1)
-            give_back(1)
         elif n == 10:
             unpack(5)
             score_quarters(2, 1, (3,))
             choose(2)
-            give_back(2)
-            give_back(3)
-            score_all(3, 1)
+            score_all(3)
         elif n == 11:
+            begin_rows(scores.at[3])
             choose(3)
-            give_back(4)
+            unpack(6)
+            score_all(4)
         elif n == 12:
-            unpack(6)
-            score_all(4, 1)
+            begin_rows(scores.at[4])
             choose(4)
-            give_back(5)
-    unpack(7)
+            unpack(7, (0,))
+            score_all(5, 0)
+    for k in range(6):
+        give_back(k)
+    unpack(7, (1,))
     score_all(5, 1)
+    begin_rows(scores.at[5])
     choose(5)
     give_back(6)
     give_back(7)
@@ -452,7 +466,7 @@
 
     def fetch(b):
         for v in range(TOPW):
-            shard, slot = w_ref[b, v], slot_of[b, v]
+            shard, slot = w_ref[v, b], slot_of[b, v]
             found = [incoming[shard, i * QB : i * QB + QB, :] for i in range(CAP)]
             found = jnp.where(slot < 0.5, found[0], jnp.where(slot < 1.5, found[1], found[2]))
             lists[v, pl.ds(pl.multiple_of(b * QB, QB), QB), :] = found
@@ -479,9 +493,7 @@
         for p in (0, 1):
             for d in range(1, NX):
                 hops[k, p, d].wait_send()
-    for n in (2, 3):
-        lib_y[n].wait_send()
-    for copy in lib_c:
+    for copy in lib_y + lib_c:
         copy.wait_send()
     for copy in returns.values():
         copy.wait_send()
@@ -522,8 +534,8 @@
             dma((8, 2, NX)),
             dma((8,)),
             dma((8,)),
-            dma((4,)),
-            dma((4,)),
+            dma((6,)),
+            dma((6,)),
             dma((4,)),
             dma((4,)),
             dma((8, NX)),
@@ -532,7 +544,7 @@
         compiler_params=pltpu.CompilerParams(
             collective_id=0, has_side_effects=True, vmem_limit_bytes=60 * 2**20
         ),
-    )(queries, library, windows)
+    )(queries, library, windows.T)
     return scores * (1.0 / math.sqrt(BINS))
 
 

time: 125 us -> 120 us (0.960)
  Pallas kernels: 121 us -> 117 us
  local copies, waits for them, and re-layouts: 1.35 us -> 0 us
    pallas_call x1, Pallas kernels: 121 us -> 117 us  [on_device(): pl.pallas_call(kernel, out_shape=jax.ShapeDtypeStruct((BLOCKS * QB, K), f...]
    unnamed x1 -> x0, local copies, waits for them, and re-layouts: 1.35 us -> none
where the time goes in v2:
time: 120 us; the launch traced here: 118 us
  Pallas kernels  117 us (98%)
  other arithmetic  1.48 us (1%)
    pallas_call x1, Pallas kernels, on_device(): pl.pallas_call(kernel, out_shape=jax.ShapeDtypeStruct((BLOCKS * QB, K), f...  117 us

profile of v2, /device:TPU:1, one launch (start us, length us, event | category | flops | bytes accessed | tf_op | source)
XLA Modules:
  0.0 118.5 jit_solution(12095994413959234075)
XLA Ops:
  0.0 117.0 %shard_map.37 = f32[128,128]{1,0:T(8,128)} custom-call(bf16[128,4096]{1,0:T(8,128)(2,1)} %q_hbm.1, bf16[192,4096]{1,0:T(8,128)(2,1)} %l_hbm.1, s32[4,16]{1,0:T(4,128)} %bitcast.1), custom_call_target="tpu_custom_call" | custom-call | tf_op jit(solution)/shard_map/pallas_call | solution.py:504
  117.0 1.5 %broadcast_multiply_fusion = f32[128,128]{1,0:T(8,128)} fusion(f32[128,128]{1,0:T(8,128)} %shard_map.37), kind=kLoop, calls=%fused_computation | loop fusion | flops 16384 | bytes 131072 | tf_op jit(solution)/shard_map/mul | solution.py:548

commit v3 on v2

--- a/solution.py
+++ b/solution.py
@@ -190,7 +190,7 @@
         pl.semaphore_signal(barrier, inc=1, device_id=((z + dz) % NZ * NX + x, r), device_id_type=MESH)
     for dx in (1, 2, 3):
         pl.semaphore_signal(barrier, inc=1, device_id=(mass_at(0, dx), r), device_id_type=MESH)
-    for dy in (1, 2, 3):
+    for dy in (1, 3):
         pl.semaphore_signal(barrier, inc=1, device_id=(m, y_rep(dy, c)), device_id_type=MESH)
     pl.semaphore_signal(barrier, inc=1, device_id=(m, y * 2 + 1 - c), device_id_type=MESH)
 
@@ -229,7 +229,7 @@
     for plane in range(NZ):
         code_own[plane] = code[plane * 8 : plane * 8 + 8]
 
-    pl.semaphore_wait(barrier, 13)
+    pl.semaphore_wait(barrier, 12)
 
     codes = {}
     for dz, dp, k in CODES:
@@ -377,7 +377,7 @@
     def score_all(group, part=None):
         repeat(2, lambda i: score(group, 1, i * (SHARD // 2), SHARD // 2, i * (SHARD // 2), part), False)
 
-    for n in range(14):
+    for n in range(12):
         if n < 10:
             ring[n].wait_send()
         else:
@@ -426,32 +426,31 @@
             score_quarters(0, 2, (1, 2))
             score_quarters(2, 1, (0, 1, 2))
         elif n == 8:
-            unpack(4)
             for group in (0, 1, 2):
                 begin_rows(scores.at[group])
         elif n == 9:
             lib_y[4].wait_recv()
             lib_y[5].wait_recv()
             lib_c[3].start()
+            unpack(4)
             lib_c[3].wait_recv()
             score_quarters(0, 2, (3,))
             choose(0)
             choose(1)
         elif n == 10:
-            unpack(5)
             score_quarters(2, 1, (3,))
             choose(2)
+            unpack(5)
             score_all(3)
         elif n == 11:
             begin_rows(scores.at[3])
             choose(3)
             unpack(6)
             score_all(4)
-        elif n == 12:
-            begin_rows(scores.at[4])
-            choose(4)
-            unpack(7, (0,))
-            score_all(5, 0)
+    begin_rows(scores.at[4])
+    choose(4)
+    unpack(7, (0,))
+    score_all(5, 0)
     for k in range(6):
         give_back(k)
     unpack(7, (1,))
@@ -489,10 +488,9 @@
 
     for copy in codes.values():
         copy.wait_send()
-    for k in range(6):
-        for p in (0, 1):
-            for d in range(1, NX):
-                hops[k, p, d].wait_send()
+    for (k, _, _), copy in hops.items():
+        if k != 6:
+            copy.wait_send()
     for copy in lib_y + lib_c:
         copy.wait_send()
     for copy in returns.values():

time: 120 us -> 121 us (level)
  Pallas kernels: 117 us -> 119 us
    pallas_call x1, Pallas kernels: 117 us -> 119 us  [on_device(): pl.pallas_call(kernel, out_shape=jax.ShapeDtypeStruct((BLOCKS * QB, K), f...]
where the time goes in v3:
time: 121 us
  Pallas kernels  119 us (98%)
  other arithmetic  1.48 us (1%)
    pallas_call x1, Pallas kernels, on_device(): pl.pallas_call(kernel, out_shape=jax.ShapeDtypeStruct((BLOCKS * QB, K), f...  119 us

profile of v3, /device:TPU:1, one launch (start us, length us, event | category | flops | bytes accessed | tf_op | source)
XLA Modules:
  0.0 120.5 jit_solution(9322873263739097708)
XLA Ops:
  0.0 119.0 %shard_map.37 = f32[128,128]{1,0:T(8,128)} custom-call(bf16[128,4096]{1,0:T(8,128)(2,1)} %q_hbm.1, bf16[192,4096]{1,0:T(8,128)(2,1)} %l_hbm.1, s32[4,16]{1,0:T(4,128)} %bitcast.1), custom_call_target="tpu_custom_call" | custom-call | tf_op jit(solution)/shard_map/pallas_call | solution.py:502
  119.0 1.5 %broadcast_multiply_fusion = f32[128,128]{1,0:T(8,128)} fusion(f32[128,128]{1,0:T(8,128)} %shard_map.37), kind=kLoop, calls=%fused_computation | loop fusion | flops 16384 | bytes 131072 | tf_op jit(solution)/shard_map/mul | solution.py:546

commit v4 on v3

--- a/solution.py
+++ b/solution.py
@@ -190,7 +190,7 @@
         pl.semaphore_signal(barrier, inc=1, device_id=((z + dz) % NZ * NX + x, r), device_id_type=MESH)
     for dx in (1, 2, 3):
         pl.semaphore_signal(barrier, inc=1, device_id=(mass_at(0, dx), r), device_id_type=MESH)
-    for dy in (1, 3):
+    for dy in (1, 2, 3):
         pl.semaphore_signal(barrier, inc=1, device_id=(m, y_rep(dy, c)), device_id_type=MESH)
     pl.semaphore_signal(barrier, inc=1, device_id=(m, y * 2 + 1 - c), device_id_type=MESH)
 
@@ -229,19 +229,20 @@
     for plane in range(NZ):
         code_own[plane] = code[plane * 8 : plane * 8 + 8]
 
-    pl.semaphore_wait(barrier, 12)
+    pl.semaphore_wait(barrier, 13)
 
     codes = {}
     for dz, dp, k in CODES:
         codes[k] = remote(
             code_own.at[(z + dp * sign + NZ) % NZ], code_in.at[k], cs.at[k], cr.at[k], (mass_at(dz, 0), r)
         )
-        codes[k].start()
 
     ring = []
     for n, (s, a, b, p) in enumerate(PIECES):
         ring.append(remote(chunk.at[a, p], chunk.at[b, p], zs.at[n], zr.at[n], (mass_at(s, 0), r)))
     ring[0].start()
+    for copy in codes.values():
+        copy.start()
 
     load_l.wait()
 
@@ -426,21 +427,21 @@
             score_quarters(0, 2, (1, 2))
             score_quarters(2, 1, (0, 1, 2))
         elif n == 8:
+            unpack(4)
             for group in (0, 1, 2):
                 begin_rows(scores.at[group])
         elif n == 9:
             lib_y[4].wait_recv()
             lib_y[5].wait_recv()
             lib_c[3].start()
-            unpack(4)
             lib_c[3].wait_recv()
             score_quarters(0, 2, (3,))
             choose(0)
             choose(1)
         elif n == 10:
+            unpack(5)
             score_quarters(2, 1, (3,))
             choose(2)
-            unpack(5)
             score_all(3)
         elif n == 11:
             begin_rows(scores.at[3])

time: 121 us -> 126 us (1.041)
  the two profiles are of different devices: /device:TPU:1 before, /device:TPU:64 now
where the time goes in v4:
time: 126 us
  Pallas kernels  124 us (98%)
  other arithmetic  1.48 us (1%)
    pallas_call x1, Pallas kernels, on_device(): pl.pallas_call(kernel, out_shape=jax.ShapeDtypeStruct((BLOCKS * QB, K), f...  124 us

profile of v4, /device:TPU:64, one launch (start us, length us, event | category | flops | bytes accessed | tf_op | source)
XLA Modules:
  0.0 125.8 jit_solution(14886214726278639183)
XLA Ops:
  0.0 124.3 %shard_map.37 = f32[128,128]{1,0:T(8,128)} custom-call(bf16[128,4096]{1,0:T(8,128)(2,1)} %q_hbm.1, bf16[192,4096]{1,0:T(8,128)(2,1)} %l_hbm.1, s32[4,16]{1,0:T(4,128)} %bitcast.1), custom_call_target="tpu_custom_call" | custom-call | tf_op jit(solution)/shard_map/pallas_call | solution.py:503
  124.3 1.5 %broadcast_multiply_fusion = f32[128,128]{1,0:T(8,128)} fusion(f32[128,128]{1,0:T(8,128)} %shard_map.37), kind=kLoop, calls=%fused_computation | loop fusion | flops 16384 | bytes 131072 | tf_op jit(solution)/shard_map/mul | solution.py:547
